TPU v7x, 768 devices: a whole 4x8x12 slice. The times are simulated.
768 devices in a mesh: row: 192 (over z, y, core), col: 4 (over x).
Axes of the slice: x: 4, y: 8, z: 12, core: 2. Of those that a mesh axis runs over, the one named last changes fastest.
Arguments:
- features: bfloat16 [24576, 128], P(('row', 'col')), may hold values from -48 to 48
- tiles: bfloat16 [18432, 128, 128], P(('row', 'col')), may hold values from -0.0546875 to 0.0546875
- tile_rows: int32 [18432], P(('row', 'col')), may hold values from 0 to 47, as said below
- tile_count: int32 [768], P(('row', 'col')), may hold values from 1 to 24, as said below
- filters: bfloat16 [4, 128, 256], replicated, may hold values from -0.25 to 0.25
Outputs:
- normalized: bfloat16 [24576, 256], P(('row', 'col'))
Inputs may be any that keep to these rules, and one draw needn't show every extreme that they name: `tile_rows`: slots at and beyond a device's count are padding. The row tiles named in one device's occupied slots are distinct. `tile_count`: some device has all 24 slots occupied.
All inputs are finite; a program needn't handle non-finite values.
Results may differ from a plain program's by a relative error of at most 0.009.
Values may be sent and summed in bfloat16 or wider, within the bound.
No kernel may reach another device: no remote copies, remote signals or barrier semaphores. Data moves between devices by JAX's collectives and lax.ppermute only.
A program may use at most 32 MiB of HBM per device.

v0:
```python
import jax
import jax.numpy as jnp
from jax import lax
from jax.sharding import PartitionSpec as P

CHEB = 4


epsilon = 1e-05


def local(features, tiles, tile_rows, tile_count, filters):
    node_rows = features.shape[0]
    in_width = features.shape[1]
    hid_width = filters.shape[2]
    slot_count = tiles.shape[0]
    tile_size = tiles.shape[1]
    row_devices = lax.axis_size("row")
    row_tiles = row_devices * node_rows // tile_size
    in_use = jnp.arange(slot_count, dtype=jnp.int32) < tile_count[0]
    matches = (tile_rows[None, :] == jnp.arange(row_tiles, dtype=jnp.int32)[:, None]) & in_use[
        None, :
    ]
    select = matches.astype(jnp.float32)

    def propagate(vector):
        gathered = lax.all_gather(vector, "col", axis=0, tiled=True)
        products = jnp.einsum("sij,jf->sif", tiles, gathered, preferred_element_type=jnp.float32)
        block_sum = jnp.einsum("ts,sif->tif", select, products, precision=lax.Precision.HIGHEST)
        block_sum = block_sum.reshape(row_tiles * tile_size, in_width)
        return lax.psum_scatter(block_sum, "row", scatter_dimension=0, tiled=True)

    cheb_terms = [features]
    cheb_terms.append(propagate(features).astype(jnp.bfloat16))
    for order in range(2, CHEB):
        image = propagate(cheb_terms[-1])
        cheb_terms.append((2.0 * image - cheb_terms[-2].astype(jnp.float32)).astype(jnp.bfloat16))
    stacked = jnp.concatenate(cheb_terms, axis=1)
    hidden = jnp.dot(stacked, filters.reshape(-1, hid_width), preferred_element_type=jnp.float32)
    total_nodes = node_rows * row_devices * lax.axis_size("col")
    col_sum = lax.psum(jnp.sum(hidden, axis=0), ("row", "col"))
    col_mean = col_sum / total_nodes
    centered = hidden - col_mean[None, :]
    spread = lax.psum(jnp.sum(centered * centered), ("row", "col")) / total_nodes
    return (centered * lax.rsqrt(spread + epsilon)).astype(jnp.bfloat16)


def solution(mesh):
    return jax.shard_map(
        local,
        mesh=mesh,
        in_specs=(
            P(("row", "col"), None),
            P(("row", "col"), None, None),
            P(("row", "col")),
            P(("row", "col")),
            P(),
        ),
        out_specs=P(("row", "col"), None),
        check_vma=False,
    )
```

profile of v0, /device:TPU:1, one launch (start us, length us, event | category | flops | bytes accessed | tf_op | source)
XLA Modules:
  0.0 1205.4 jit_solution(8598746619349164757)
XLA Ops:
  6.5 0.0 copy-start
  6.5 0.0 copy-start.4
  6.5 0.0 reduce-scatter.4.cloned.1.call-start
  7.3 10.4 all_gather.9
  17.7 1.9 fusion.8
  19.6 0.0 copy-done.4
  19.6 1.5 fusion.25
  21.1 2.6 copy.6
  23.8 0.0 copy-start.1
  23.8 0.0 reduce-scatter.4.cloned.1.call-update
  23.8 0.0 reduce-scatter.6.cloned.1.call-start
  23.8 315.4 %reduce-scatter.4.cloned.1.call-done = f32[32,128]{1,0:T(8,128)} async-done(((f32[6144,128]{1,0:T(8,128)}), f32[32,128]{1,0:T(8,128)}) %reduce-scatter.4.cloned.1.call-update) | async-done | bytes 16400 | tf_op jit(solution)/shard_map/reduce_scatter | solution.py:31
  339.3 0.7 convert_element_type.19
  340.0 9.3 all_gather.10
  349.3 0.0 copy-done.1
  349.3 0.6 fusion.6
  349.9 1.5 fusion.2
  351.4 2.6 copy.7
  354.1 0.0 copy-start.2
  354.1 0.0 reduce-scatter.6.cloned.1.call-update
  354.1 0.0 reduce-scatter.8.cloned.1.call-start
  354.2 307.1 %reduce-scatter.6.cloned.1.call-done = f32[32,128]{1,0:T(8,128)} async-done(((f32[6144,128]{1,0:T(8,128)}), f32[32,128]{1,0:T(8,128)}) %reduce-scatter.6.cloned.1.call-update) | async-done | bytes 16400 | tf_op jit(solution)/shard_map/reduce_scatter | solution.py:31
  661.2 0.0 copy-done.2
  661.2 0.7 subtract_convert_fusion.1
  661.9 9.3 all_gather.11
  671.3 0.6 fusion.4
  671.9 1.5 fusion
  673.4 2.6 copy.8
  676.0 0.0 copy-start.3
  676.0 0.0 reduce-scatter.8.cloned.1.call-update
  676.1 307.1 %reduce-scatter.8.cloned.1.call-done = f32[32,128]{1,0:T(8,128)} async-done(((f32[6144,128]{1,0:T(8,128)}), f32[32,128]{1,0:T(8,128)}) %reduce-scatter.8.cloned.1.call-update) | async-done | bytes 16400 | tf_op jit(solution)/shard_map/reduce_scatter | solution.py:31
  983.2 0.0 copy-done.3
  983.2 0.7 subtract_convert_fusion
  983.9 0.0 copy-done
  983.9 0.2 fusion.34
  984.1 108.9 %psum.14 = f32[256]{0:T(256)S(1)} all-reduce(f32[256]{0:T(256)S(1)} %get-tuple-element.5), channel_id=1, replica_groups=mesh['row'=192,'col'=4] {'row','col'}, use_global_device_ids=true, to_apply=%region_4.0 | all-reduce | flops 256 | bytes 2048 | tf_op jit(solution)/shard_map/psum | solution.py:41
  1093.0 0.6 multiply_reduce_fusion
  1093.6 104.0 %psum.15 = f32[]{:T(128)} all-reduce(f32[]{:T(128)} %multiply_reduce_fusion), channel_id=1, replica_groups=mesh['row'=192,'col'=4] {'row','col'}, use_global_device_ids=true, to_apply=%region_6.0 | all-reduce | flops 1 | bytes 8 | tf_op jit(solution)/shard_map/psum | solution.py:44
  1198.2 0.6 multiply_convert_fusion
  (2 shorter events, 0.0 us)
Async XLA Ops:
  6.5 977.4 %copy-start = (bf16[4,128,256]{2,1,0:T(8,128)(2,1)S(1)}, bf16[4,128,256]{2,1,0:T(8,128)(2,1)}, u32[]{:S(2)}) copy-start(bf16[4,128,256]{2,1,0:T(8,128)(2,1)} %param.9) | copy-start | bytes 786436
  6.5 13.0 %copy-start.4 = (s32[24]{0:T(128)S(1)}, s32[24]{0:T(128)}, u32[]{:S(2)}) copy-start(s32[24]{0:T(128)} %param.7) | copy-start | bytes 292
  6.5 332.7 %reduce-scatter.4.cloned.1.call-start = ((), (), s32[]{:S(2)}) async-start(), calls=%async_computation.3 | async-start | bytes 3162112 | tf_op jit(solution)/shard_map/reduce_scatter | solution.py:31
  23.8 325.5 %copy-start.1 = (bf16[24,128,128]{2,1,0:T(8,128)(2,1)S(1)}, bf16[24,128,128]{2,1,0:T(8,128)(2,1)}, u32[]{:S(2)}) copy-start(bf16[24,128,128]{2,1,0:T(8,128)(2,1)} %param.6) | copy-start | bytes 2359300
  23.8 637.4 %reduce-scatter.6.cloned.1.call-start = ((), (), s32[]{:S(2)}) async-start(), calls=%async_computation.4 | async-start | bytes 3162112 | tf_op jit(solution)/shard_map/reduce_scatter | solution.py:31
  354.1 307.1 %copy-start.2 = (bf16[32,128]{1,0:T(8,128)(2,1)S(1)}, bf16[32,128]{1,0:T(8,128)(2,1)}, u32[]{:S(2)}) copy-start(bf16[32,128]{1,0:T(8,128)(2,1)} %param.5) | copy-start | bytes 24580
  354.1 629.1 %reduce-scatter.8.cloned.1.call-start = ((), (), s32[]{:S(2)}) async-start(), calls=%async_computation.5 | async-start | bytes 3162112 | tf_op jit(solution)/shard_map/reduce_scatter | solution.py:31
  676.0 307.2 %copy-start.3 = (f32[32,128]{1,0:T(8,128)S(1)}, f32[32,128]{1,0:T(8,128)}, u32[]{:S(2)}) copy-start(f32[32,128]{1,0:T(8,128)} %reduce-scatter.4.cloned.1.call-done) | copy-start | bytes 49156
Sparse Core Ops, SparseCore 0:
  23.9 315.3 reduce-scatter.3
  354.2 306.9 reduce-scatter.5
  676.2 306.9 reduce-scatter.7
where the time goes:
time: 1210 us
  waiting for transfers between devices  930 us (77%)
  blocking collectives  242 us (20%)
  between operations  14.6 us (1%)
    reduce_scatter x3, waiting for transfers between devices, propagate(): return lax.psum_scatter(block_sum, 'row', scatter_dimension=0, tiled=True)  930 us
    psum x1, blocking collectives, local(): col_sum = lax.psum(jnp.sum(hidden, axis=0), ('row', 'col'))  109 us
    psum x1, blocking collectives, local(): lax.psum(jnp.sum(centered * centered), ('row', 'col')) / total_nodes  104 us
    all_gather x3, blocking collectives, propagate(): gathered = lax.all_gather(vector, 'col', axis=0, tiled=True)  29.1 us
  transfers between devices with their start and end apart: 3, of which 3 were waited for; matrix products, arithmetic and copies ran while one was open for 0% of the time, Pallas kernels for 0%

commit v1 on v0

v1 whole, which is shorter than its diff:
```python
import functools
import jax
import jax.numpy as jnp
from jax import lax
from jax.experimental import pallas as pl
from jax.experimental.pallas import tpu as pltpu
from jax.sharding import Mesh
from jax.sharding import PartitionSpec as P

VM = pl.BlockSpec(memory_space=pltpu.VMEM)
SM = pl.BlockSpec(memory_space=pltpu.SMEM)
epsilon = 1e-05
MODE = "yz"


def place_kernel(y_size, y_first, rows_ref, count_ref, tiles_ref, *out_refs):
    parts = len(out_refs)
    rows = out_refs[0].shape[3]
    pieces = tiles_ref.shape[1] // (rows * parts)
    for out_ref in out_refs:
        out_ref[...] = jnp.zeros_like(out_ref)

    def put(slot, carry):
        first = rows_ref[slot] * pieces
        for q in range(pieces):
            chip = (first + q) // 2
            y, z = chip % y_size, chip // y_size
            for part, out_ref in enumerate(out_refs):
                start = (q * parts + part) * rows
                place = (y, z) if y_first[part] else (z, y)
                out_ref[(first + q) % 2, place[0], place[1]] = tiles_ref[slot, start : start + rows, :]
        return carry

    lax.fori_loop(0, count_ref[0], put, 0)


def place(tiles, tile_rows, tile_count, z_size, y_size, piece, y_first):
    rows, cols = piece // len(y_first), tiles.shape[2]
    shapes = [(2, y_size, z_size, rows, cols) if y else (2, z_size, y_size, rows, cols) for y in y_first]
    return pl.pallas_call(
        functools.partial(place_kernel, y_size, y_first),
        out_shape=[jax.ShapeDtypeStruct(s, tiles.dtype) for s in shapes],
        in_specs=[SM, SM, VM],
        out_specs=[VM] * len(shapes),
        compiler_params=pltpu.CompilerParams(vmem_limit_bytes=16 * 1024 * 1024),
    )(tile_rows, tile_count, tiles)


def sum_kernel(in_ref, out_ref):
    for i in range(in_ref.shape[1]):
        total = in_ref[0, i].astype(jnp.float32)
        for source in range(1, in_ref.shape[0]):
            total = total + in_ref[source, i].astype(jnp.float32)
        total = total.astype(out_ref.dtype)
        for copy in range(out_ref.shape[1]):
            out_ref[i, copy] = total


def sum_sources(array, copies):
    return pl.pallas_call(
        sum_kernel,
        out_shape=jax.ShapeDtypeStruct((array.shape[1], copies) + array.shape[2:], array.dtype),
        in_specs=[VM],
        out_specs=VM,
    )(array)


def term_kernel(parts, scale, *refs):
    in_refs, prev_ref, out_ref = refs[:parts], (refs[parts] if scale != 1.0 else None), refs[-1]
    rows = in_refs[0].shape[2]
    for i in range(out_ref.shape[0]):
        for part, in_ref in enumerate(in_refs):
            total = in_ref[0, i].astype(jnp.float32)
            for source in range(1, in_ref.shape[0]):
                total = total + in_ref[source, i].astype(jnp.float32)
            at = slice(part * rows, (part + 1) * rows)
            if scale != 1.0:
                total = scale * total - prev_ref[i, at].astype(jnp.float32)
            out_ref[i, at] = total.astype(out_ref.dtype)


def next_term(parts, prev):
    operands = list(parts) + ([prev] if prev is not None else [])
    shape = (parts[0].shape[1], parts[0].shape[2] * len(parts), parts[0].shape[3])
    return pl.pallas_call(
        functools.partial(term_kernel, len(parts), 1.0 if prev is None else 2.0),
        out_shape=jax.ShapeDtypeStruct(shape, parts[0].dtype),
        in_specs=[VM] * len(operands),
        out_specs=VM,
    )(*operands)


def spread_out(piece, axes):
    size = lax.axis_size(axes)
    return lax.all_to_all(jnp.broadcast_to(piece, (size,) + piece.shape), axes, 0, 0, tiled=True)


def merge(stats, axes, nodes):
    gathered = spread_out(stats, axes)
    means, squares = gathered[:, :2], gathered[:, 2:]
    mean = jnp.mean(means, axis=0)
    off = means - mean[None]
    return jnp.concatenate([mean, jnp.sum(squares + nodes * (off * off), axis=0)], axis=0)


def local(features, tiles, tile_rows, tile_count, filters):
    piece, width = features.shape
    hid_width = filters.shape[2]
    z_size, y_size, x_size = lax.axis_size("z"), lax.axis_size("y"), lax.axis_size("x")
    x_index = lax.axis_index("x")

    y_first = {"yz": (True,), "zy": (False,), "split": (True, False)}[MODE]
    rows = piece // len(y_first)
    matrices = []
    for dense in place(tiles, tile_rows, tile_count, z_size, y_size, piece, y_first):
        swapped = lax.all_to_all(dense, "core", 0, 0, tiled=True)
        matrices.append(jnp.concatenate([swapped[0], swapped[1]], axis=-1).reshape(-1, 2 * tiles.shape[2]))

    def propagate(vector, copies):
        parts = []
        for y, matrix in zip(y_first, matrices):
            one, two = ("y", "z") if y else ("z", "y")
            products = jnp.dot(matrix, vector, preferred_element_type=jnp.float32).astype(jnp.bfloat16)
            products = products.reshape(lax.axis_size(one), lax.axis_size(two), rows, width)
            received = lax.all_to_all(products, one, 0, 0, tiled=True)
            summed = sum_sources(received, copies)
            summed = summed.reshape(-1, rows, width)
            received = lax.all_to_all(summed, (two, "x") if copies > 1 else two, 0, 0, tiled=True)
            parts.append(received.reshape(lax.axis_size(two), copies, rows, width))
        return parts

    def both_cores(half):
        return lax.all_gather(half.reshape(-1, width), "core", axis=0, tiled=True)

    def own(array):
        return lax.dynamic_index_in_dim(array, x_index, 0, keepdims=False)

    gathered = spread_out(features, ("core", "x"))
    half0 = lax.dynamic_slice_in_dim(gathered, lax.axis_index("core") * x_size, x_size, 0)
    half1 = next_term(propagate(gathered.reshape(-1, width), x_size), None)
    half2 = next_term(propagate(both_cores(half1), x_size), half0)
    own1 = own(half1)
    term3 = next_term(propagate(both_cores(half2), 1), own1[None])[0]
    stacked = jnp.concatenate([features, own1, own(half2), term3], axis=1)
    hidden = jnp.dot(stacked, filters.reshape(-1, hid_width), preferred_element_type=jnp.float32)

    mean = jnp.mean(hidden, axis=0)
    off = hidden - mean[None, :]
    stats = jnp.stack([mean, jnp.sum(off * off, axis=0)]).reshape(4, hid_width // 2)
    nodes = piece
    for axes in ("y", "z", ("core", "x")):
        stats = merge(stats, axes, float(nodes))
        nodes = nodes * lax.axis_size(axes)
    spread = jnp.sum(stats[2:]) / nodes
    centered = hidden - stats[:2].reshape(1, hid_width)
    return (centered * lax.rsqrt(spread + epsilon)).astype(jnp.bfloat16)


def split_of(row_devices):
    y_size = 8
    return row_devices // (2 * y_size), y_size


def solution(mesh):
    cols = mesh.shape["col"]
    z_size, y_size = split_of(mesh.shape["row"])
    fine = Mesh(mesh.devices.reshape(z_size, y_size, 2, cols), ("z", "y", "core", "x"))
    rows = ("z", "y", "core", "x")
    return jax.shard_map(
        local,
        mesh=fine,
        in_specs=(P(rows, None), P(rows, None, None), P(rows), P(rows), P()),
        out_specs=P(rows, None),
        check_vma=False,
    )
```

time: 1210 us -> 240 us (0.20)
  waiting for transfers between devices: 930 us -> 56.2 us
  blocking collectives: 242 us -> 141 us
  starting transfers between devices: 0.09 us -> 15.8 us
  between operations: 14.6 us -> 1.53 us
  Pallas kernels: 0 us -> 12.6 us
    reduce_scatter x3 -> x0, waiting for transfers between devices: 930 us -> none  [propagate(): return lax.psum_scatter(block_sum, 'row', scatter_dimension=0, tiled=True)]
    psum x2 -> x0, blocking collectives: 213 us -> none  [the longest x1 109 us: local(): col_sum = lax.psum(jnp.sum(hidden, axis=0), ('row', 'col'))]
    all_to_all x0 -> x7, blocking collectives: none -> 131 us  [the longest x2 53.3 us: propagate(): received = lax.all_to_all(products, one, 0, 0, tiled=True)]
    all_to_all x0 -> x4, waiting for transfers between devices: none -> 56.2 us  [the longest x2 28 us: propagate(): lax.all_to_all(summed, (two, 'x') if copies > 1 else two, 0, 0, tiled=True)]
    all_gather x3 -> x2, blocking collectives: 29.1 us -> 9.85 us  [both_cores(): return lax.all_gather(half.reshape(-1, width), 'core', axis=0, tiled=True)]
    all_to_all x0 -> x4, starting transfers between devices: none -> 15.8 us  [the longest x2 8.45 us: propagate(): lax.all_to_all(summed, (two, 'x') if copies > 1 else two, 0, 0, tiled=True)]
    pallas_call x0 -> x7, Pallas kernels: none -> 12.6 us  [the longest x3 5.83 us: sum_sources(): pl.pallas_call(sum_kernel, out_shape=jax.ShapeDtypeStruct((array.shape[1]...]
  transfers between devices with their start and end apart: 3 -> 4, of which waited for: 3 -> 4; matrix products, arithmetic and copies ran while one was open for 0% -> 1% of each run, Pallas kernels for 0% -> 0%
where the time goes in v1:
time: 240 us; the launch traced here: 239 us
  blocking collectives  141 us (59%)
  waiting for transfers between devices  56.2 us (23%)
  starting transfers between devices  15.8 us (7%)
  Pallas kernels  12.6 us (5%)
  local copies, waits for them, and re-layouts  6.95 us (3%)
  matrix products  3.44 us (1%)
    all_to_all x2, blocking collectives, propagate(): received = lax.all_to_all(products, one, 0, 0, tiled=True)  53.3 us
    all_to_all x3, blocking collectives, spread_out(): lax.all_to_all(jnp.broadcast_to(piece, (size,) + piece.shape), axes, 0, 0...  33.3 us
    all_to_all x1, blocking collectives, propagate(): lax.all_to_all(summed, (two, 'x') if copies > 1 else two, 0, 0, tiled=True)  29.4 us
    all_to_all x2, waiting for transfers between devices, propagate(): lax.all_to_all(summed, (two, 'x') if copies > 1 else two, 0, 0, tiled=True)  28 us
    all_to_all x1, waiting for transfers between devices, propagate(): received = lax.all_to_all(products, one, 0, 0, tiled=True)  23.6 us
    all_to_all x1, blocking collectives, local(): swapped = lax.all_to_all(dense, 'core', 0, 0, tiled=True)  15.1 us
    all_gather x2, blocking collectives, both_cores(): return lax.all_gather(half.reshape(-1, width), 'core', axis=0, tiled=True)  9.85 us
    all_to_all x2, starting transfers between devices, propagate(): lax.all_to_all(summed, (two, 'x') if copies > 1 else two, 0, 0, tiled=True)  8.45 us
  transfers between devices with their start and end apart: 4, of which 4 were waited for; matrix products, arithmetic and copies ran while one was open for 1% of the time, Pallas kernels for 0%

profile of v1, /device:TPU:1, one launch (start us, length us, event | category | flops | bytes accessed | tf_op | source)
XLA Modules:
  0.0 238.8 jit_solution(7906231859483730703)
XLA Ops:
  0.0 0.0 copy-start
  0.7 0.0 copy-start.1
  0.7 1.1 copy-done.1
  1.8 0.0 copy-start.2
  1.8 0.7 copy-done.2
  2.5 2.0 shard_map.55
  4.5 0.0 copy-start.7
  4.5 15.1 %all_to_all.55 = bf16[2,8,12,32,128]{4,3,2,1,0:T(8,128)(2,1)S(1)} all-to-all(bf16[2,8,12,32,128]{4,3,2,1,0:T(8,128)(2,1)S(1)} %shard_map.55), channel_id=1, replica_groups=mesh['z'=12,'y'=8,'core'=2,'x'=4] {'core'}, dimensions={0} | all-to-all | bytes 3145728 | tf_op jit(solution)/shard_map/all_to_all | solution.py:116
  19.6 0.0 copy-done.7
  19.6 0.6 broadcast_in_dim.8
  20.2 3.6 %all-to-all-start.1 = ((bf16[8,32,128]{2,1,0:T(8,128)(2,1)}), bf16[8,32,128]{2,1,0:T(8,128)(2,1)S(1)}, u32[]{:S(2)}, u32[]{:S(2)}) async-start(bf16[8,32,128]{2,1,0:T(8,128)(2,1)} %broadcast_in_dim.8), calls=%async_computation.1 | async-start | bytes 131072 | tf_op jit(solution)/shard_map/all_to_all | solution.py:95
  23.8 0.3 fusion.20
  24.2 4.6 %all-to-all-done.1 = bf16[8,32,128]{2,1,0:T(8,128)(2,1)S(1)} async-done(((bf16[8,32,128]{2,1,0:T(8,128)(2,1)}), bf16[8,32,128]{2,1,0:T(8,128)(2,1)S(1)}, u32[]{:S(2)}, u32[]{:S(2)}) %all-to-all-start.1) | async-done | bytes 65568 | tf_op jit(solution)/shard_map/all_to_all | solution.py:95
  28.8 0.6 convolution_convert_fusion.2
  29.3 26.6 %all_to_all.56.in_ref = bf16[8,12,32,128]{3,2,1,0:T(8,128)(2,1)} all-to-all(bf16[8,12,32,128]{3,2,1,0:T(8,128)(2,1)S(1)} %bitcast.34), channel_id=1, replica_groups=mesh['z'=12,'y'=8,'core'=2,'x'=4] {'y'}, dimensions={0} | all-to-all | bytes 1572864 | tf_op jit(solution)/shard_map/all_to_all | solution.py:125
  56.0 2.0 shard_map.56
  58.0 29.4 %all_to_all.57 = bf16[48,32,128]{2,1,0:T(8,128)(2,1)} all-to-all(bf16[48,32,128]{2,1,0:T(8,128)(2,1)} %bitcast.32), channel_id=1, replica_groups=mesh['z'=12,'y'=8,'core'=2,'x'=4] {'z','x'}, dimensions={0} | all-to-all | bytes 786432 | tf_op jit(solution)/shard_map/all_to_all | solution.py:128
  87.4 1.6 shard_map.57
  89.0 5.4 %all_gather.6 = bf16[256,128]{1,0:T(8,128)(2,1)S(1)} all-gather(bf16[128,128]{1,0:T(8,128)(2,1)} %bitcast.43), channel_id=1, replica_groups=mesh['z'=12,'y'=8,'core'=2,'x'=4] {'core'}, dimensions={0}, use_global_device_ids=true | all-gather | bytes 98304 | tf_op jit(solution)/shard_map/all_gather | solution.py:133
  94.4 0.6 convolution_convert_fusion.1
  95.0 26.7 %all_to_all.58.in_ref = bf16[8,12,32,128]{3,2,1,0:T(8,128)(2,1)} all-to-all(bf16[8,12,32,128]{3,2,1,0:T(8,128)(2,1)S(1)} %bitcast.33), channel_id=1, replica_groups=mesh['z'=12,'y'=8,'core'=2,'x'=4] {'y'}, dimensions={0} | all-to-all | bytes 1572864 | tf_op jit(solution)/shard_map/all_to_all | solution.py:125
  121.6 2.0 shard_map.58
  123.6 4.9 %all-to-all-start.5 = ((bf16[48,32,128]{2,1,0:T(8,128)(2,1)}), bf16[48,32,128]{2,1,0:T(8,128)(2,1)S(1)}, u32[]{:S(2)}, u32[]{:S(2)}) async-start(bf16[48,32,128]{2,1,0:T(8,128)(2,1)} %bitcast.31), calls=%async_computation.5 | async-start | bytes 786432 | tf_op jit(solution)/shard_map/all_to_all | solution.py:128
  128.6 0.6 constant_dynamic-slice_fusion.refs_1_
  129.2 19.3 %all-to-all-done.5 = bf16[48,32,128]{2,1,0:T(8,128)(2,1)S(1)} async-done(((bf16[48,32,128]{2,1,0:T(8,128)(2,1)}), bf16[48,32,128]{2,1,0:T(8,128)(2,1)S(1)}, u32[]{:S(2)}, u32[]{:S(2)}) %all-to-all-start.5) | async-done | bytes 393248 | tf_op jit(solution)/shard_map/all_to_all | solution.py:128
  148.5 0.0 copy-start.4
  148.5 0.7 copy-done.4
  149.2 1.7 shard_map.59
  150.9 4.5 %all_gather.7 = bf16[256,128]{1,0:T(8,128)(2,1)S(1)} all-gather(bf16[128,128]{1,0:T(8,128)(2,1)} %bitcast.44), channel_id=1, replica_groups=mesh['z'=12,'y'=8,'core'=2,'x'=4] {'core'}, dimensions={0}, use_global_device_ids=true | all-gather | bytes 98304 | tf_op jit(solution)/shard_map/all_gather | solution.py:133
  155.3 1.5 convolution_convert_fusion
  156.8 3.7 %all-to-all-start.6 = ((bf16[8,12,32,128]{3,2,1,0:T(8,128)(2,1)}), bf16[8,12,32,128]{3,2,1,0:T(8,128)(2,1)S(1)}, u32[]{:S(2)}, u32[]{:S(2)}) async-start(bf16[8,12,32,128]{3,2,1,0:T(8,128)(2,1)} %bitcast.13), calls=%async_computation.6 | async-start | bytes 1572864 | tf_op jit(solution)/shard_map/all_to_all | solution.py:125
  160.5 23.6 %all-to-all-done.6.in_ref = bf16[8,12,32,128]{3,2,1,0:T(8,128)(2,1)S(1)} async-done(((bf16[8,12,32,128]{3,2,1,0:T(8,128)(2,1)}), bf16[8,12,32,128]{3,2,1,0:T(8,128)(2,1)S(1)}, u32[]{:S(2)}, u32[]{:S(2)}) %all-to-all-start.6) | async-done | bytes 786464 | tf_op jit(solution)/shard_map/all_to_all | solution.py:125
  184.0 0.9 copy-done.3
  184.9 1.9 shard_map.60
  186.8 3.5 %all-to-all-start.7 = ((bf16[12,32,128]{2,1,0:T(8,128)(2,1)}), bf16[12,32,128]{2,1,0:T(8,128)(2,1)S(1)}, u32[]{:S(2)}, u32[]{:S(2)}) async-start(bf16[12,32,128]{2,1,0:T(8,128)(2,1)} %bitcast.42), calls=%async_computation.7 | async-start | bytes 196608 | tf_op jit(solution)/shard_map/all_to_all | solution.py:128
  190.3 0.0 copy-done.6
  190.3 0.6 constant_dynamic-slice_fusion.1.refs_1_
  190.9 0.7 dynamic-slice_bitcast_fusion
  191.6 8.7 %all-to-all-done.7 = bf16[12,32,128]{2,1,0:T(8,128)(2,1)S(1)} async-done(((bf16[12,32,128]{2,1,0:T(8,128)(2,1)}), bf16[12,32,128]{2,1,0:T(8,128)(2,1)S(1)}, u32[]{:S(2)}, u32[]{:S(2)}) %all-to-all-start.7) | async-done | bytes 98336 | tf_op jit(solution)/shard_map/all_to_all | solution.py:128
  200.4 0.6 copy-done.5
  201.0 1.5 shard_map.61
  202.5 0.0 copy-done
  202.5 0.9 fusion.21
  203.4 9.0 %all_to_all.59 = f32[8,4,128]{2,1,0:T(4,128)S(1)} all-to-all(f32[8,4,128]{2,1,0:T(4,128)S(1)} %broadcast_in_dim.18), channel_id=1, replica_groups=mesh['z'=12,'y'=8,'core'=2,'x'=4] {'y'}, dimensions={0} | all-to-all | bytes 32768 | tf_op jit(solution)/shard_map/all_to_all | solution.py:95
  212.5 12.5 %all_to_all.60 = f32[12,4,128]{2,1,0:T(4,128)S(1)} all-to-all(f32[12,4,128]{2,1,0:T(4,128)S(1)} %broadcast_in_dim.19), channel_id=1, replica_groups=mesh['z'=12,'y'=8,'core'=2,'x'=4] {'z'}, dimensions={0} | all-to-all | bytes 49152 | tf_op jit(solution)/shard_map/all_to_all | solution.py:95
  225.1 11.9 %all_to_all.61 = f32[8,4,128]{2,1,0:T(4,128)S(1)} all-to-all(f32[8,4,128]{2,1,0:T(4,128)S(1)} %broadcast_in_dim.20), channel_id=1, replica_groups=mesh['z'=12,'y'=8,'core'=2,'x'=4] {'core','x'}, dimensions={0} | all-to-all | bytes 32768 | tf_op jit(solution)/shard_map/all_to_all | solution.py:95
  236.9 0.6 fusion.9
  238.2 0.6 multiply_convert_fusion
  (21 shorter events, 0.2 us)
Async XLA Ops:
  0.0 202.5 %copy-start = (bf16[4,128,256]{2,1,0:T(8,128)(2,1)S(1)}, bf16[4,128,256]{2,1,0:T(8,128)(2,1)}, u32[]{:S(2)}) copy-start(bf16[4,128,256]{2,1,0:T(8,128)(2,1)} %param.9) | copy-start | bytes 786436
  0.7 1.1 copy-start.1
  1.8 0.7 copy-start.2
  4.5 15.1 %copy-start.7 = (bf16[32,128]{1,0:T(8,128)(2,1)S(1)}, bf16[32,128]{1,0:T(8,128)(2,1)}, u32[]{:S(2)}) copy-start(bf16[32,128]{1,0:T(8,128)(2,1)} %param.5) | copy-start | bytes 24580
  20.2 8.6 %all-to-all-start.1 = ((bf16[8,32,128]{2,1,0:T(8,128)(2,1)}), bf16[8,32,128]{2,1,0:T(8,128)(2,1)S(1)}, u32[]{:S(2)}, u32[]{:S(2)}) async-start(bf16[8,32,128]{2,1,0:T(8,128)(2,1)} %broadcast_in_dim.8), calls=%async_computation.1 | async-start | bytes 131072 | tf_op jit(solution)/shard_map/all_to_all | solution.py:95
  123.6 24.8 %all-to-all-start.5 = ((bf16[48,32,128]{2,1,0:T(8,128)(2,1)}), bf16[48,32,128]{2,1,0:T(8,128)(2,1)S(1)}, u32[]{:S(2)}, u32[]{:S(2)}) async-start(bf16[48,32,128]{2,1,0:T(8,128)(2,1)} %bitcast.31), calls=%async_computation.5 | async-start | bytes 786432 | tf_op jit(solution)/shard_map/all_to_all | solution.py:128
  148.5 0.7 copy-start.4
  156.8 33.5 %copy-start.6 = (bf16[4,32,128]{2,1,0:T(8,128)(2,1)S(1)}, bf16[4,32,128]{2,1,0:T(8,128)(2,1)}, u32[]{:S(2)}) copy-start(bf16[4,32,128]{2,1,0:T(8,128)(2,1)} %shard_map.57) | copy-start | bytes 98308
  156.8 27.2 %all-to-all-start.6 = ((bf16[8,12,32,128]{3,2,1,0:T(8,128)(2,1)}), bf16[8,12,32,128]{3,2,1,0:T(8,128)(2,1)S(1)}, u32[]{:S(2)}, u32[]{:S(2)}) async-start(bf16[8,12,32,128]{3,2,1,0:T(8,128)(2,1)} %bitcast.13), calls=%async_computation.6 | async-start | bytes 1572864 | tf_op jit(solution)/shard_map/all_to_all | solution.py:125
  184.0 0.9 copy-start.3
  186.8 13.6 %all-to-all-start.7 = ((bf16[12,32,128]{2,1,0:T(8,128)(2,1)}), bf16[12,32,128]{2,1,0:T(8,128)(2,1)S(1)}, u32[]{:S(2)}, u32[]{:S(2)}) async-start(bf16[12,32,128]{2,1,0:T(8,128)(2,1)} %bitcast.42), calls=%async_computation.7 | async-start | bytes 196608 | tf_op jit(solution)/shard_map/all_to_all | solution.py:128
  200.3 0.6 copy-start.5

commit v2 on v0

v2 whole, which is shorter than its diff:
```python
import jax
import jax.numpy as jnp
from jax import lax
from jax.experimental import pallas as pl
from jax.experimental.pallas import tpu as pltpu
from jax.sharding import Mesh
from jax.sharding import PartitionSpec as P

VM = pl.BlockSpec(memory_space=pltpu.VMEM)
SM = pl.BlockSpec(memory_space=pltpu.SMEM)
CORES = 2
ALL = "device"
epsilon = 1e-05


class Layout:
    def __init__(self, zs, ys, xs):
        self.zs, self.ys, self.xs = zs, ys, xs
        self.members = 2 * 2 * CORES
        self.squares = zs * ys // 4
        at = lambda z, y, core, x: ((z * ys + y) * CORES + core) * xs + x
        Z, Y, C, X, B = range(zs), range(ys), range(CORES), range(xs), range(2)
        corners = [(z, y) for z in range(0, zs, 2) for y in range(0, ys, 2)]
        member = [(core, y, z) for core in C for y in B for z in B]
        self.square = [[at(z + j, y + i, core, x) for core, i, j in member] for z, y in corners for x in X]
        self.square_line = [[at(z + j, y + i, core, x) for core, i, j in member for x in X] for z, y in corners]
        self.across = [[at(z + j, y + i, core, x) for z, y in corners] for core, i, j in member for x in X]
        self.y_x = [[at(z, y, core, x) for y in Y for x in X] for z in Z for core in C]
        self.z_core = [[at(z, y, core, x) for z in Z for core in C] for y in Y for x in X]

    def place_of(self, core, chip):
        z, y = chip // self.ys, chip % self.ys
        return (core * 2 + y % 2) * 2 + z % 2, (z // 2) * (self.ys // 2) + y // 2


def exchange(array, groups):
    return lax.all_to_all(array, ALL, 0, 0, axis_index_groups=groups, tiled=True)


def place(layout, tiles, tile_rows, tile_count, piece):
    def kernel(rows_ref, count_ref, tiles_ref, out_ref):
        pieces = tiles_ref.shape[1] // piece
        out_ref[...] = jnp.zeros_like(out_ref)

        def put(slot, carry):
            first = rows_ref[slot] * pieces
            for q in range(pieces):
                member, square = layout.place_of(q % CORES, (first + q) // CORES)
                out_ref[member, square] = tiles_ref[slot, q * piece : (q + 1) * piece, :]
            return carry

        lax.fori_loop(0, count_ref[0], put, 0)

    return pl.pallas_call(
        kernel,
        out_shape=jax.ShapeDtypeStruct((layout.members, layout.squares, piece, tiles.shape[2]), tiles.dtype),
        in_specs=[SM, SM, VM],
        out_specs=VM,
        compiler_params=pltpu.CompilerParams(vmem_limit_bytes=16 * 1024 * 1024),
    )(tile_rows, tile_count, tiles)


def total_of(ref, *at):
    total = ref[(0, *at)].astype(jnp.float32)
    for source in range(1, ref.shape[0]):
        total = total + ref[(source, *at)].astype(jnp.float32)
    return total


def next_term(partial, prev, copies):
    def kernel(in_ref, *refs):
        out_ref = refs[-1]
        term = total_of(in_ref)
        if prev is not None:
            term = 2.0 * term - refs[0][...].astype(jnp.float32)
        for copy in range(copies):
            out_ref[copy] = term.astype(out_ref.dtype)

    operands = [partial] if prev is None else [partial, prev]
    return pl.pallas_call(
        kernel,
        out_shape=jax.ShapeDtypeStruct((copies,) + partial.shape[1:], partial.dtype),
        in_specs=[VM] * len(operands),
        out_specs=VM,
    )(*operands)


def merge(stats, groups, nodes):
    gathered = exchange(jnp.broadcast_to(stats, (len(groups[0]),) + stats.shape), groups)
    means, squares = gathered[:, :2], gathered[:, 2:]
    mean = jnp.mean(means, axis=0)
    off = means - mean[None]
    return jnp.concatenate([mean, jnp.sum(squares + nodes * (off * off), axis=0)], axis=0)


def local_of(layout):
    def local(features, tiles, tile_rows, tile_count, filters):
        piece, width = features.shape
        hid_width = filters.shape[2]
        copies = layout.members * layout.xs

        def gather(pieces):
            return exchange(pieces, layout.square_line).reshape(-1, width)

        vector = gather(jnp.broadcast_to(features, (copies,) + features.shape))
        dense = place(layout, tiles, tile_rows, tile_count, piece)
        dense, vector = lax.optimization_barrier((dense, vector))
        swapped = exchange(dense, layout.square).reshape(layout.members, -1, tiles.shape[2])
        matrix = jnp.concatenate([swapped[i] for i in range(layout.members)], axis=-1)

        def propagate(vector):
            products = jnp.dot(matrix, vector, preferred_element_type=jnp.float32).astype(jnp.bfloat16)
            return exchange(products.reshape(layout.squares, piece, width), layout.across)

        pieces1 = next_term(propagate(vector), None, copies)
        pieces2 = next_term(propagate(gather(pieces1)), features, copies)
        term3 = next_term(propagate(gather(pieces2)), pieces1[0], 1)[0]
        stacked = jnp.concatenate([features, pieces1[0], pieces2[0], term3], axis=1)
        hidden = jnp.dot(stacked, filters.reshape(-1, hid_width), preferred_element_type=jnp.float32)

        mean = jnp.mean(hidden, axis=0)
        off = hidden - mean[None, :]
        stats = jnp.stack([mean, jnp.sum(off * off, axis=0)]).reshape(4, hid_width // 2)
        nodes = piece
        for groups in (layout.y_x, layout.z_core):
            stats = merge(stats, groups, float(nodes))
            nodes = nodes * len(groups[0])
        spread = jnp.sum(stats[2:]) / nodes
        centered = hidden - stats[:2].reshape(1, hid_width)
        return (centered * lax.rsqrt(spread + epsilon)).astype(jnp.bfloat16)

    return local


def split_of(row_devices):
    return row_devices // (8 * CORES), 8


def solution(mesh):
    zs, ys = split_of(mesh.shape["row"])
    line = Mesh(mesh.devices.reshape(-1), (ALL,))
    return jax.shard_map(
        local_of(Layout(zs, ys, mesh.shape["col"])),
        mesh=line,
        in_specs=(P(ALL, None), P(ALL, None, None), P(ALL), P(ALL), P()),
        out_specs=P(ALL, None),
        check_vma=False,
    )
```

time: 1210 us -> 189 us (0.16)
  waiting for transfers between devices: 930 us -> 18.8 us
  blocking collectives: 242 us -> 131 us
  starting transfers between devices: 0.09 us -> 18 us
  between operations: 14.6 us -> 1.5 us
    reduce_scatter x3 -> x0, waiting for transfers between devices: 930 us -> none  [propagate(): return lax.psum_scatter(block_sum, 'row', scatter_dimension=0, tiled=True)]
    psum x2 -> x0, blocking collectives: 213 us -> none  [the longest x1 109 us: local(): col_sum = lax.psum(jnp.sum(hidden, axis=0), ('row', 'col'))]
    all_to_all x0 -> x7, blocking collectives: none -> 131 us  [exchange(): lax.all_to_all(array, ALL, 0, 0, axis_index_groups=groups, tiled=True)]
    all_gather x3 -> x0, blocking collectives: 29.1 us -> none  [propagate(): gathered = lax.all_gather(vector, 'col', axis=0, tiled=True)]
    all_to_all x0 -> x2, waiting for transfers between devices: none -> 18.8 us  [exchange(): lax.all_to_all(array, ALL, 0, 0, axis_index_groups=groups, tiled=True)]
    all_to_all x0 -> x2, starting transfers between devices: none -> 18 us  [exchange(): lax.all_to_all(array, ALL, 0, 0, axis_index_groups=groups, tiled=True)]
  transfers between devices with their start and end apart: 3 -> 2, of which waited for: 3 -> 2; matrix products, arithmetic and copies ran while one was open for 0% -> 1% of each run, Pallas kernels for 0% -> 1%
where the time goes in v2:
time: 189 us; the launch traced here: 188 us
  blocking collectives  131 us (69%)
  waiting for transfers between devices  18.8 us (10%)
  starting transfers between devices  18 us (10%)
  local copies, waits for them, and re-layouts  6.73 us (4%)
  Pallas kernels  6.57 us (3%)
  matrix products  3.28 us (2%)
    all_to_all x7, blocking collectives, exchange(): lax.all_to_all(array, ALL, 0, 0, axis_index_groups=groups, tiled=True)  131 us
    all_to_all x2, waiting for transfers between devices, exchange(): lax.all_to_all(array, ALL, 0, 0, axis_index_groups=groups, tiled=True)  18.8 us
    all_to_all x2, starting transfers between devices, exchange(): lax.all_to_all(array, ALL, 0, 0, axis_index_groups=groups, tiled=True)  18 us
    pallas_call x3, Pallas kernels, next_term(): pl.pallas_call(kernel, out_shape=jax.ShapeDtypeStruct((copies,) + partial...  4.89 us
  transfers between devices with their start and end apart: 2, of which 2 were waited for; matrix products, arithmetic and copies ran while one was open for 1% of the time, Pallas kernels for 1%

profile of v2, /device:TPU:1, one launch (start us, length us, event | category | flops | bytes accessed | tf_op | source)
XLA Modules:
  0.0 187.6 jit_solution(6208436889685260452)
XLA Ops:
  0.0 0.0 copy-start
  0.0 1.5 broadcast_in_dim.12
  1.5 14.1 %all-to-all-start = ((bf16[32,32,128]{2,1,0:T(8,128)(2,1)}), bf16[32,32,128]{2,1,0:T(8,128)(2,1)S(1)}, u32[]{:S(2)}, u32[]{:S(2)}) async-start(bf16[32,32,128]{2,1,0:T(8,128)(2,1)} %broadcast_in_dim.12), calls=%async_computation | async-start | bytes 524288 | tf_op jit(solution)/shard_map/all_to_all | solution.py:37
  16.3 0.0 copy-start.1
  16.3 1.1 copy-done.1
  17.4 0.0 copy-start.2
  17.4 0.7 copy-done.2
  18.1 1.7 shard_map.55
  19.7 3.5 %all-to-all-done = bf16[32,32,128]{2,1,0:T(8,128)(2,1)S(1)} async-done(((bf16[32,32,128]{2,1,0:T(8,128)(2,1)}), bf16[32,32,128]{2,1,0:T(8,128)(2,1)S(1)}, u32[]{:S(2)}, u32[]{:S(2)}) %all-to-all-start) | async-done | bytes 262176 | tf_op jit(solution)/shard_map/all_to_all | solution.py:37
  23.3 24.0 %all_to_all.45 = bf16[8,24,32,128]{3,2,1,0:T(8,128)(2,1)S(1)} all-to-all(bf16[8,24,32,128]{3,2,1,0:T(8,128)(2,1)S(1)} %shard_map.55), channel_id=1, replica_groups={{0,64,8,72,4,68,12,76},{1,65,9,73,5,69,13,77},{2,66,10,74,6,70,14,78},{..., dimensions={0} | all-to-all | bytes 3145728 | tf_op jit(solution)/shard_map/all_to_all | solution.py:37
  47.3 0.3 fusion.16
  47.6 0.1 constant_dynamic-update-slice_fusion.6
  47.7 0.1 constant_dynamic-update-slice_fusion.5
  47.7 0.1 constant_dynamic-update-slice_fusion.4
  47.8 0.1 constant_dynamic-update-slice_fusion.3
  47.9 0.1 constant_dynamic-update-slice_fusion.2
  48.0 0.1 constant_dynamic-update-slice_fusion.1
  48.0 0.1 constant_dynamic-update-slice_fusion
  48.1 0.6 convolution_convert_fusion.2
  48.7 30.5 %all_to_all.46.in_ref = bf16[24,32,128]{2,1,0:T(8,128)(2,1)} all-to-all(bf16[24,32,128]{2,1,0:T(8,128)(2,1)S(1)} %bitcast.43), channel_id=1, replica_groups={{0,16,32,48,128,144,160,176,256,272,288,304,384,400,416,432,512,528,544..., dimensions={0} | all-to-all | bytes 393216 | tf_op jit(solution)/shard_map/all_to_all | solution.py:37
  79.1 1.7 shard_map.56
  80.8 13.1 %all_to_all.47 = bf16[32,32,128]{2,1,0:T(8,128)(2,1)S(1)} all-to-all(bf16[32,32,128]{2,1,0:T(8,128)(2,1)} %shard_map.56), channel_id=1, replica_groups={{0,1,2,3,64,65,66,67,8,9,10,11,72,73,74,75,4,5,6,7,68,69,70,71,12,13,14..., dimensions={0} | all-to-all | bytes 524288 | tf_op jit(solution)/shard_map/all_to_all | solution.py:37
  93.9 0.6 convolution_convert_fusion.1
  94.4 20.9 %all_to_all.48.in_ref = bf16[24,32,128]{2,1,0:T(8,128)(2,1)} all-to-all(bf16[24,32,128]{2,1,0:T(8,128)(2,1)S(1)} %bitcast.44), channel_id=1, replica_groups={{0,16,32,48,128,144,160,176,256,272,288,304,384,400,416,432,512,528,544..., dimensions={0} | all-to-all | bytes 393216 | tf_op jit(solution)/shard_map/all_to_all | solution.py:37
  115.4 1.7 shard_map.57
  117.0 0.0 copy-start.4
  117.0 14.1 %all_to_all.49 = bf16[32,32,128]{2,1,0:T(8,128)(2,1)S(1)} all-to-all(bf16[32,32,128]{2,1,0:T(8,128)(2,1)} %shard_map.57), channel_id=1, replica_groups={{0,1,2,3,64,65,66,67,8,9,10,11,72,73,74,75,4,5,6,7,68,69,70,71,12,13,14..., dimensions={0} | all-to-all | bytes 524288 | tf_op jit(solution)/shard_map/all_to_all | solution.py:37
  131.1 1.3 convolution_convert_fusion
  132.4 3.8 %all-to-all-start.6 = ((bf16[24,32,128]{2,1,0:T(8,128)(2,1)}), bf16[24,32,128]{2,1,0:T(8,128)(2,1)S(1)}, u32[]{:S(2)}, u32[]{:S(2)}) async-start(bf16[24,32,128]{2,1,0:T(8,128)(2,1)} %bitcast.15), calls=%async_computation.6 | async-start | bytes 393216 | tf_op jit(solution)/shard_map/all_to_all | solution.py:37
  136.2 1.3 slice_bitcast_fusion.1.refs_0_
  137.5 0.7 slice_bitcast_fusion
  138.2 15.3 %all-to-all-done.6.in_ref = bf16[24,32,128]{2,1,0:T(8,128)(2,1)S(1)} async-done(((bf16[24,32,128]{2,1,0:T(8,128)(2,1)}), bf16[24,32,128]{2,1,0:T(8,128)(2,1)S(1)}, u32[]{:S(2)}, u32[]{:S(2)}) %all-to-all-start.6) | async-done | bytes 196640 | tf_op jit(solution)/shard_map/all_to_all | solution.py:37
  153.5 0.0 copy-start.3
  153.5 0.7 copy-done.3
  154.2 1.6 shard_map.58
  155.7 0.0 copy-done
  155.7 0.0 copy-done.4
  155.7 0.9 fusion.17
  156.7 12.3 %all_to_all.50 = f32[32,4,128]{2,1,0:T(4,128)S(1)} all-to-all(f32[32,4,128]{2,1,0:T(4,128)S(1)} %broadcast_in_dim.13), channel_id=1, replica_groups={{0,1,2,3,8,9,10,11,16,17,18,19,24,25,26,27,32,33,34,35,40,41,42,43,48,4..., dimensions={0} | all-to-all | bytes 131072 | tf_op jit(solution)/shard_map/all_to_all | solution.py:37
  169.1 16.6 %all_to_all.51 = f32[24,4,128]{2,1,0:T(4,128)S(1)} all-to-all(f32[24,4,128]{2,1,0:T(4,128)S(1)} %broadcast_in_dim.14), channel_id=1, replica_groups={{0,4,64,68,128,132,192,196,256,260,320,324,384,388,448,452,512,516,576,..., dimensions={0} | all-to-all | bytes 98304 | tf_op jit(solution)/shard_map/all_to_all | solution.py:37
  185.7 0.6 fusion.11
  187.0 0.6 multiply_convert_fusion
  (13 shorter events, 0.3 us)
Async XLA Ops:
  0.0 155.7 %copy-start = (bf16[4,128,256]{2,1,0:T(8,128)(2,1)S(1)}, bf16[4,128,256]{2,1,0:T(8,128)(2,1)}, u32[]{:S(2)}) copy-start(bf16[4,128,256]{2,1,0:T(8,128)(2,1)} %param.9) | copy-start | bytes 786436
  1.5 21.8 %all-to-all-start = ((bf16[32,32,128]{2,1,0:T(8,128)(2,1)}), bf16[32,32,128]{2,1,0:T(8,128)(2,1)S(1)}, u32[]{:S(2)}, u32[]{:S(2)}) async-start(bf16[32,32,128]{2,1,0:T(8,128)(2,1)} %broadcast_in_dim.12), calls=%async_computation | async-start | bytes 524288 | tf_op jit(solution)/shard_map/all_to_all | solution.py:37
  16.3 1.1 copy-start.1
  17.4 0.7 copy-start.2
  117.0 38.7 %copy-start.4 = (bf16[32,128]{1,0:T(8,128)(2,1)S(1)}, bf16[32,128]{1,0:T(8,128)(2,1)}, u32[]{:S(2)}) copy-start(bf16[32,128]{1,0:T(8,128)(2,1)} %refs_0_.1) | copy-start | bytes 24580
  132.4 21.1 %all-to-all-start.6 = ((bf16[24,32,128]{2,1,0:T(8,128)(2,1)}), bf16[24,32,128]{2,1,0:T(8,128)(2,1)S(1)}, u32[]{:S(2)}, u32[]{:S(2)}) async-start(bf16[24,32,128]{2,1,0:T(8,128)(2,1)} %bitcast.15), calls=%async_computation.6 | async-start | bytes 393216 | tf_op jit(solution)/shard_map/all_to_all | solution.py:37
  153.5 0.7 copy-start.3

commit v3 on v2

--- a/solution.py
+++ b/solution.py
@@ -60,29 +60,13 @@
     )(tile_rows, tile_count, tiles)
 
 
-def total_of(ref, *at):
-    total = ref[(0, *at)].astype(jnp.float32)
-    for source in range(1, ref.shape[0]):
-        total = total + ref[(source, *at)].astype(jnp.float32)
-    return total
-
-
-def next_term(partial, prev, copies):
-    def kernel(in_ref, *refs):
-        out_ref = refs[-1]
-        term = total_of(in_ref)
-        if prev is not None:
-            term = 2.0 * term - refs[0][...].astype(jnp.float32)
-        for copy in range(copies):
-            out_ref[copy] = term.astype(out_ref.dtype)
-
-    operands = [partial] if prev is None else [partial, prev]
-    return pl.pallas_call(
-        kernel,
-        out_shape=jax.ShapeDtypeStruct((copies,) + partial.shape[1:], partial.dtype),
-        in_specs=[VM] * len(operands),
-        out_specs=VM,
-    )(*operands)
+def next_term(partial, prev):
+    term = partial[0].astype(jnp.float32)
+    for source in range(1, partial.shape[0]):
+        term = term + partial[source].astype(jnp.float32)
+    if prev is not None:
+        term = 2.0 * term - prev.astype(jnp.float32)
+    return term.astype(partial.dtype)
 
 
 def merge(stats, groups, nodes):
@@ -99,10 +83,11 @@
         hid_width = filters.shape[2]
         copies = layout.members * layout.xs
 
-        def gather(pieces):
+        def gather(piece_rows):
+            pieces = jnp.broadcast_to(piece_rows, (copies,) + piece_rows.shape)
             return exchange(pieces, layout.square_line).reshape(-1, width)
 
-        vector = gather(jnp.broadcast_to(features, (copies,) + features.shape))
+        vector = gather(features)
         dense = place(layout, tiles, tile_rows, tile_count, piece)
         dense, vector = lax.optimization_barrier((dense, vector))
         swapped = exchange(dense, layout.square).reshape(layout.members, -1, tiles.shape[2])
@@ -112,10 +97,10 @@
             products = jnp.dot(matrix, vector, preferred_element_type=jnp.float32).astype(jnp.bfloat16)
             return exchange(products.reshape(layout.squares, piece, width), layout.across)
 
-        pieces1 = next_term(propagate(vector), None, copies)
-        pieces2 = next_term(propagate(gather(pieces1)), features, copies)
-        term3 = next_term(propagate(gather(pieces2)), pieces1[0], 1)[0]
-        stacked = jnp.concatenate([features, pieces1[0], pieces2[0], term3], axis=1)
+        term1 = next_term(propagate(vector), None)
+        term2 = next_term(propagate(gather(term1)), features)
+        term3 = next_term(propagate(gather(term2)), term1)
+        stacked = jnp.concatenate([features, term1, term2, term3], axis=1)
         hidden = jnp.dot(stacked, filters.reshape(-1, hid_width), preferred_element_type=jnp.float32)
 
         mean = jnp.mean(hidden, axis=0)

time: 189 us -> 179 us (0.947)
  blocking collectives: 131 us -> 150 us
  waiting for transfers between devices: 18.8 us -> 2.22 us
  starting transfers between devices: 18 us -> 14.1 us
  Pallas kernels: 6.57 us -> 3 us
  local copies, waits for them, and re-layouts: 6.73 us -> 4.14 us
    all_to_all x7 -> x8, blocking collectives: 131 us -> 150 us  [exchange(): lax.all_to_all(array, ALL, 0, 0, axis_index_groups=groups, tiled=True)]
    all_to_all x2 -> x1, waiting for transfers between devices: 18.8 us -> 2.22 us  [exchange(): lax.all_to_all(array, ALL, 0, 0, axis_index_groups=groups, tiled=True)]
    pallas_call x3 -> x0, Pallas kernels: 4.89 us -> none  [next_term(): pl.pallas_call(kernel, out_shape=jax.ShapeDtypeStruct((copies,) + partial...]
    all_to_all x2 -> x1, starting transfers between devices: 18 us -> 14.1 us  [exchange(): lax.all_to_all(array, ALL, 0, 0, axis_index_groups=groups, tiled=True)]
    squeeze x2 -> x0, local copies, waits for them, and re-layouts: 1.99 us -> none  [local(): stacked = jnp.concatenate([features, pieces1[0], pieces2[0], term3], axis=1)]
  transfers between devices with their start and end apart: 2 -> 1, of which waited for: 2 -> 1; matrix products, arithmetic and copies ran while one was open for 1% -> 0% of each run, Pallas kernels for 1% -> 2%
where the time goes in v3:
time: 179 us; the launch traced here: 178 us
  blocking collectives  150 us (84%)
  starting transfers between devices  14.1 us (8%)
  local copies, waits for them, and re-layouts  4.14 us (2%)
  Pallas kernels  3 us (2%)
  waiting for transfers between devices  2.22 us (1%)
  matrix products  1.88 us (1%)
    all_to_all x8, blocking collectives, exchange(): lax.all_to_all(array, ALL, 0, 0, axis_index_groups=groups, tiled=True)  150 us
    all_to_all x1, starting transfers between devices, exchange(): lax.all_to_all(array, ALL, 0, 0, axis_index_groups=groups, tiled=True)  14.1 us
  transfers between devices with their start and end apart: 1, of which 1 were waited for; matrix products, arithmetic and copies ran while one was open for 0% of the time, Pallas kernels for 2%

profile of v3, /device:TPU:1, one launch (start us, length us, event | category | flops | bytes accessed | tf_op | source)
XLA Modules:
  0.0 178.2 jit_solution(7559274881768078633)
XLA Ops:
  0.0 0.0 copy-start
  0.0 1.5 broadcast_in_dim.18
  1.5 14.1 %all-to-all-start = ((bf16[32,32,128]{2,1,0:T(8,128)(2,1)}), bf16[32,32,128]{2,1,0:T(8,128)(2,1)S(1)}, u32[]{:S(2)}, u32[]{:S(2)}) async-start(bf16[32,32,128]{2,1,0:T(8,128)(2,1)} %broadcast_in_dim.18), calls=%async_computation | async-start | bytes 524288 | tf_op jit(solution)/shard_map/all_to_all | solution.py:37
  16.3 0.0 copy-start.1
  16.3 1.1 copy-done.1
  17.4 0.0 copy-start.2
  17.4 0.7 copy-done.2
  18.1 3.0 %shard_map.55 = bf16[8,24,32,128]{3,2,1,0:T(8,128)(2,1)S(1)} custom-call(s32[24]{0:T(128)S(1)} %copy-done.2, s32[1]{0:T(128)S(6)} %copy.47.count_ref, bf16[24,128,128]{2,1,0:T(8,128)(2,1)S(1)} %copy-done.1), custom_call_target="tpu_custom_call" | custom-call | tf_op jit(solution)/shard_map/pallas_call | solution.py:54
  21.1 2.2 %all-to-all-done = bf16[32,32,128]{2,1,0:T(8,128)(2,1)S(1)} async-done(((bf16[32,32,128]{2,1,0:T(8,128)(2,1)}), bf16[32,32,128]{2,1,0:T(8,128)(2,1)S(1)}, u32[]{:S(2)}, u32[]{:S(2)}) %all-to-all-start) | async-done | bytes 262176 | tf_op jit(solution)/shard_map/all_to_all | solution.py:37
  23.3 24.0 %all_to_all.45 = bf16[8,24,32,128]{3,2,1,0:T(8,128)(2,1)S(1)} all-to-all(bf16[8,24,32,128]{3,2,1,0:T(8,128)(2,1)S(1)} %shard_map.55), channel_id=1, replica_groups={{0,64,8,72,4,68,12,76},{1,65,9,73,5,69,13,77},{2,66,10,74,6,70,14,78},{..., dimensions={0} | all-to-all | bytes 3145728 | tf_op jit(solution)/shard_map/all_to_all | solution.py:37
  47.3 0.3 fusion.23
  47.6 0.1 constant_dynamic-update-slice_fusion.6
  47.7 0.1 constant_dynamic-update-slice_fusion.5
  47.7 0.1 constant_dynamic-update-slice_fusion.4
  47.8 0.1 constant_dynamic-update-slice_fusion.3
  47.9 0.1 constant_dynamic-update-slice_fusion.2
  48.0 0.1 constant_dynamic-update-slice_fusion.1
  48.0 0.1 constant_dynamic-update-slice_fusion
  48.1 0.6 convolution_convert_fusion.2
  48.7 30.4 %all_to_all.46 = bf16[24,32,128]{2,1,0:T(8,128)(2,1)S(1)} all-to-all(bf16[24,32,128]{2,1,0:T(8,128)(2,1)S(1)} %bitcast.200), channel_id=1, replica_groups={{0,16,32,48,128,144,160,176,256,272,288,304,384,400,416,432,512,528,544..., dimensions={0} | all-to-all | bytes 393216 | tf_op jit(solution)/shard_map/all_to_all | solution.py:37
  79.1 0.0 copy-start.3
  79.1 12.5 %all_to_all.47 = bf16[32,32,128]{2,1,0:T(8,128)(2,1)S(1)} all-to-all(bf16[32,32,128]{2,1,0:T(8,128)(2,1)S(1)} %broadcast_in_dim.19), channel_id=1, replica_groups={{0,1,2,3,64,65,66,67,8,9,10,11,72,73,74,75,4,5,6,7,68,69,70,71,12,13,14..., dimensions={0} | all-to-all | bytes 524288 | tf_op jit(solution)/shard_map/all_to_all | solution.py:37
  91.7 0.6 convolution_convert_fusion.1
  92.2 20.2 %all_to_all.48 = bf16[24,32,128]{2,1,0:T(8,128)(2,1)S(1)} all-to-all(bf16[24,32,128]{2,1,0:T(8,128)(2,1)S(1)} %bitcast.201), channel_id=1, replica_groups={{0,16,32,48,128,144,160,176,256,272,288,304,384,400,416,432,512,528,544..., dimensions={0} | all-to-all | bytes 393216 | tf_op jit(solution)/shard_map/all_to_all | solution.py:37
  112.4 0.0 copy-done.3
  112.5 13.7 %all_to_all.49 = bf16[32,32,128]{2,1,0:T(8,128)(2,1)S(1)} all-to-all(bf16[32,32,128]{2,1,0:T(8,128)(2,1)S(1)} %broadcast_in_dim.20), channel_id=1, replica_groups={{0,1,2,3,64,65,66,67,8,9,10,11,72,73,74,75,4,5,6,7,68,69,70,71,12,13,14..., dimensions={0} | all-to-all | bytes 524288 | tf_op jit(solution)/shard_map/all_to_all | solution.py:37
  126.2 0.6 convolution_convert_fusion
  126.7 20.2 %all_to_all.50 = bf16[24,32,128]{2,1,0:T(8,128)(2,1)S(1)} all-to-all(bf16[24,32,128]{2,1,0:T(8,128)(2,1)S(1)} %bitcast.199), channel_id=1, replica_groups={{0,16,32,48,128,144,160,176,256,272,288,304,384,400,416,432,512,528,544..., dimensions={0} | all-to-all | bytes 393216 | tf_op jit(solution)/shard_map/all_to_all | solution.py:37
  146.9 0.1 fusion.16
  147.0 0.0 copy-done
  147.0 0.2 fusion.24
  147.3 12.4 %all_to_all.51 = f32[32,4,128]{2,1,0:T(4,128)S(1)} all-to-all(f32[32,4,128]{2,1,0:T(4,128)S(1)} %broadcast_in_dim.21), channel_id=1, replica_groups={{0,1,2,3,8,9,10,11,16,17,18,19,24,25,26,27,32,33,34,35,40,41,42,43,48,4..., dimensions={0} | all-to-all | bytes 131072 | tf_op jit(solution)/shard_map/all_to_all | solution.py:37
  159.8 16.5 %all_to_all.52 = f32[24,4,128]{2,1,0:T(4,128)S(1)} all-to-all(f32[24,4,128]{2,1,0:T(4,128)S(1)} %broadcast_in_dim.22), channel_id=1, replica_groups={{0,4,64,68,128,132,192,196,256,260,320,324,384,388,448,452,512,516,576,..., dimensions={0} | all-to-all | bytes 98304 | tf_op jit(solution)/shard_map/all_to_all | solution.py:37
  176.3 0.6 fusion.11
  177.6 0.6 multiply_convert_fusion
  (17 shorter events, 0.4 us)
Async XLA Ops:
  0.0 147.0 %copy-start = (bf16[4,128,256]{2,1,0:T(8,128)(2,1)S(1)}, bf16[4,128,256]{2,1,0:T(8,128)(2,1)}, u32[]{:S(2)}) copy-start(bf16[4,128,256]{2,1,0:T(8,128)(2,1)} %param.9) | copy-start | bytes 786436
  1.5 21.8 %all-to-all-start = ((bf16[32,32,128]{2,1,0:T(8,128)(2,1)}), bf16[32,32,128]{2,1,0:T(8,128)(2,1)S(1)}, u32[]{:S(2)}, u32[]{:S(2)}) async-start(bf16[32,32,128]{2,1,0:T(8,128)(2,1)} %broadcast_in_dim.18), calls=%async_computation | async-start | bytes 524288 | tf_op jit(solution)/shard_map/all_to_all | solution.py:37
  16.3 1.1 copy-start.1
  17.4 0.7 copy-start.2
  79.1 33.3 %copy-start.3 = (bf16[32,128]{1,0:T(8,128)(2,1)S(1)}, bf16[32,128]{1,0:T(8,128)(2,1)}, u32[]{:S(2)}) copy-start(bf16[32,128]{1,0:T(8,128)(2,1)} %param.5) | copy-start | bytes 24580

commit v4 on v3

--- a/solution.py
+++ b/solution.py
@@ -20,9 +20,10 @@
         self.squares = zs * ys // 4
         at = lambda z, y, core, x: ((z * ys + y) * CORES + core) * xs + x
         Z, Y, C, X, B = range(zs), range(ys), range(CORES), range(xs), range(2)
-        corners = [(z, y) for z in range(0, zs, 2) for y in range(0, ys, 2)]
+        corners = [(z, y) for y in range(0, ys, 2) for z in range(0, zs, 2)]
         member = [(core, y, z) for core in C for y in B for z in B]
         self.square = [[at(z + j, y + i, core, x) for core, i, j in member] for z, y in corners for x in X]
+        self.x_line = [[at(z, y, core, x) for x in X] for z in Z for y in Y for core in C]
         self.square_line = [[at(z + j, y + i, core, x) for core, i, j in member for x in X] for z, y in corners]
         self.across = [[at(z + j, y + i, core, x) for z, y in corners] for core, i, j in member for x in X]
         self.y_x = [[at(z, y, core, x) for y in Y for x in X] for z in Z for core in C]
@@ -30,7 +31,7 @@
 
     def place_of(self, core, chip):
         z, y = chip // self.ys, chip % self.ys
-        return (core * 2 + y % 2) * 2 + z % 2, (z // 2) * (self.ys // 2) + y // 2
+        return (core * 2 + y % 2) * 2 + z % 2, (y // 2) * (self.zs // 2) + z // 2
 
 
 def exchange(array, groups):
@@ -87,9 +88,12 @@
             pieces = jnp.broadcast_to(piece_rows, (copies,) + piece_rows.shape)
             return exchange(pieces, layout.square_line).reshape(-1, width)
 
-        vector = gather(features)
+        in_square = jnp.broadcast_to(features, (layout.members,) + features.shape)
+        in_square = exchange(in_square, layout.square)
         dense = place(layout, tiles, tile_rows, tile_count, piece)
-        dense, vector = lax.optimization_barrier((dense, vector))
+        dense, in_square = lax.optimization_barrier((dense, in_square))
+        vector = lax.all_gather(in_square, ALL, axis=0, axis_index_groups=layout.x_line)
+        vector = jnp.swapaxes(vector, 0, 1).reshape(-1, width)
         swapped = exchange(dense, layout.square).reshape(layout.members, -1, tiles.shape[2])
         matrix = jnp.concatenate([swapped[i] for i in range(layout.members)], axis=-1)
 

time: 179 us -> 176 us (0.983)
  blocking collectives: 150 us -> 133 us
  waiting for transfers between devices: 2.22 us -> 10.8 us
  starting transfers between devices: 14.1 us -> 18.5 us
    all_to_all x8 -> x7, blocking collectives: 150 us -> 124 us  [exchange(): lax.all_to_all(array, ALL, 0, 0, axis_index_groups=groups, tiled=True)]
    all_gather x0 -> x1, blocking collectives: none -> 9.5 us  [local(): lax.all_gather(in_square, ALL, axis=0, axis_index_groups=layout.x_line)]
    all_to_all x1 -> x2, waiting for transfers between devices: 2.22 us -> 10.8 us  [exchange(): lax.all_to_all(array, ALL, 0, 0, axis_index_groups=groups, tiled=True)]
    all_to_all x1 -> x2, starting transfers between devices: 14.1 us -> 18.5 us  [exchange(): lax.all_to_all(array, ALL, 0, 0, axis_index_groups=groups, tiled=True)]
  transfers between devices with their start and end apart: 1 -> 2, of which waited for: 1 -> 1; matrix products, arithmetic and copies ran while one was open for 0% -> 0% of each run, Pallas kernels for 2% -> 2%
where the time goes in v4:
time: 176 us; the launch traced here: 175 us
  blocking collectives  133 us (76%)
  starting transfers between devices  18.5 us (11%)
  waiting for transfers between devices  10.8 us (6%)
  local copies, waits for them, and re-layouts  4.05 us (2%)
  Pallas kernels  3.5 us (2%)
  matrix products  1.89 us (1%)
    all_to_all x7, blocking collectives, exchange(): lax.all_to_all(array, ALL, 0, 0, axis_index_groups=groups, tiled=True)  124 us
    all_to_all x2, starting transfers between devices, exchange(): lax.all_to_all(array, ALL, 0, 0, axis_index_groups=groups, tiled=True)  18.5 us
    all_to_all x2, waiting for transfers between devices, exchange(): lax.all_to_all(array, ALL, 0, 0, axis_index_groups=groups, tiled=True)  10.8 us
    all_gather x1, blocking collectives, local(): lax.all_gather(in_square, ALL, axis=0, axis_index_groups=layout.x_line)  9.5 us
  transfers between devices with their start and end apart: 2, of which 1 were waited for; matrix products, arithmetic and copies ran while one was open for 0% of the time, Pallas kernels for 2%

profile of v4, /device:TPU:1, one launch (start us, length us, event | category | flops | bytes accessed | tf_op | source)
XLA Modules:
  0.0 175.3 jit_solution(10112823702691938565)
XLA Ops:
  0.0 0.0 copy-start
  0.0 1.4 broadcast_in_dim.18
  1.4 13.8 %all-to-all-start = ((bf16[8,32,128]{2,1,0:T(8,128)(2,1)}), bf16[8,32,128]{2,1,0:T(8,128)(2,1)S(1)}, u32[]{:S(2)}, u32[]{:S(2)}) async-start(bf16[8,32,128]{2,1,0:T(8,128)(2,1)} %broadcast_in_dim.18), calls=%async_computation | async-start | bytes 131072 | tf_op jit(solution)/shard_map/all_to_all | solution.py:38
  15.8 0.0 copy-start.1
  15.8 1.1 copy-done.1
  16.9 0.0 copy-start.2
  16.9 0.7 copy-done.2
  17.6 3.5 %shard_map.55 = bf16[8,24,32,128]{3,2,1,0:T(8,128)(2,1)} custom-call(s32[24]{0:T(128)S(1)} %copy-done.2, s32[1]{0:T(128)S(6)} %copy.52.count_ref, bf16[24,128,128]{2,1,0:T(8,128)(2,1)S(1)} %copy-done.1), custom_call_target="tpu_custom_call" | custom-call | tf_op jit(solution)/shard_map/pallas_call | solution.py:55
  21.1 0.0 all-to-all-done
  21.1 4.8 %all-to-all-start.1 = ((bf16[8,24,32,128]{3,2,1,0:T(8,128)(2,1)}), bf16[8,24,32,128]{3,2,1,0:T(8,128)(2,1)S(1)}, u32[]{:S(2)}, u32[]{:S(2)}) async-start(bf16[8,24,32,128]{3,2,1,0:T(8,128)(2,1)} %shard_map.55), calls=%async_computation.1 | async-start | bytes 3145728 | tf_op jit(solution)/shard_map/all_to_all | solution.py:38
  25.9 9.5 %all-gather = bf16[32,32,128]{2,1,0:T(8,128)(2,1)S(1)} all-gather(bf16[8,32,128]{2,1,0:T(8,128)(2,1)S(1)} %all-to-all-done), channel_id=2, replica_groups={{0,1,2,3},{4,5,6,7},{8,9,10,11},{12,13,14,15},{16,17,18,19},{20,21,22,2..., dimensions={0}, use_global_device_ids=true | all-gather | bytes 327680 | tf_op jit(solution)/shard_map/all_gather | solution.py:95
  35.4 10.8 %all-to-all-done.1 = bf16[8,24,32,128]{3,2,1,0:T(8,128)(2,1)S(1)} async-done(((bf16[8,24,32,128]{3,2,1,0:T(8,128)(2,1)}), bf16[8,24,32,128]{3,2,1,0:T(8,128)(2,1)S(1)}, u32[]{:S(2)}, u32[]{:S(2)}) %all-to-all-start.1) | async-done | bytes 1572896 | tf_op jit(solution)/shard_map/all_to_all | solution.py:38
  46.2 0.3 fusion.23
  46.5 0.1 constant_dynamic-update-slice_fusion.6
  46.6 0.1 constant_dynamic-update-slice_fusion.5
  46.6 0.1 constant_dynamic-update-slice_fusion.4
  46.7 0.1 constant_dynamic-update-slice_fusion.3
  46.8 0.1 constant_dynamic-update-slice_fusion.2
  46.8 0.1 constant_dynamic-update-slice_fusion.1
  46.9 0.1 constant_dynamic-update-slice_fusion
  47.0 0.6 convolution_convert_fusion.2
  47.6 26.3 %all_to_all.45 = bf16[24,32,128]{2,1,0:T(8,128)(2,1)S(1)} all-to-all(bf16[24,32,128]{2,1,0:T(8,128)(2,1)S(1)} %bitcast.204), channel_id=1, replica_groups={{0,128,256,384,512,640,16,144,272,400,528,656,32,160,288,416,544,672,48..., dimensions={0} | all-to-all | bytes 393216 | tf_op jit(solution)/shard_map/all_to_all | solution.py:38
  73.9 0.0 copy-start.3
  74.0 14.5 %all_to_all.46 = bf16[32,32,128]{2,1,0:T(8,128)(2,1)S(1)} all-to-all(bf16[32,32,128]{2,1,0:T(8,128)(2,1)S(1)} %broadcast_in_dim.19), channel_id=1, replica_groups={{0,1,2,3,64,65,66,67,8,9,10,11,72,73,74,75,4,5,6,7,68,69,70,71,12,13,14..., dimensions={0} | all-to-all | bytes 524288 | tf_op jit(solution)/shard_map/all_to_all | solution.py:38
  88.5 0.6 convolution_convert_fusion.1
  89.1 19.5 %all_to_all.47 = bf16[24,32,128]{2,1,0:T(8,128)(2,1)S(1)} all-to-all(bf16[24,32,128]{2,1,0:T(8,128)(2,1)S(1)} %bitcast.205), channel_id=1, replica_groups={{0,128,256,384,512,640,16,144,272,400,528,656,32,160,288,416,544,672,48..., dimensions={0} | all-to-all | bytes 393216 | tf_op jit(solution)/shard_map/all_to_all | solution.py:38
  108.5 0.0 copy-done.3
  108.6 14.3 %all_to_all.48 = bf16[32,32,128]{2,1,0:T(8,128)(2,1)S(1)} all-to-all(bf16[32,32,128]{2,1,0:T(8,128)(2,1)S(1)} %broadcast_in_dim.20), channel_id=1, replica_groups={{0,1,2,3,64,65,66,67,8,9,10,11,72,73,74,75,4,5,6,7,68,69,70,71,12,13,14..., dimensions={0} | all-to-all | bytes 524288 | tf_op jit(solution)/shard_map/all_to_all | solution.py:38
  122.9 0.6 convolution_convert_fusion
  123.5 19.2 %all_to_all.49 = bf16[24,32,128]{2,1,0:T(8,128)(2,1)S(1)} all-to-all(bf16[24,32,128]{2,1,0:T(8,128)(2,1)S(1)} %bitcast.203), channel_id=1, replica_groups={{0,128,256,384,512,640,16,144,272,400,528,656,32,160,288,416,544,672,48..., dimensions={0} | all-to-all | bytes 393216 | tf_op jit(solution)/shard_map/all_to_all | solution.py:38
  142.6 0.1 fusion.16
  142.7 0.0 copy-done
  142.7 0.2 fusion.24
  143.0 14.0 %all_to_all.50 = f32[32,4,128]{2,1,0:T(4,128)S(1)} all-to-all(f32[32,4,128]{2,1,0:T(4,128)S(1)} %broadcast_in_dim.21), channel_id=1, replica_groups={{0,1,2,3,8,9,10,11,16,17,18,19,24,25,26,27,32,33,34,35,40,41,42,43,48,4..., dimensions={0} | all-to-all | bytes 131072 | tf_op jit(solution)/shard_map/all_to_all | solution.py:38
  157.1 16.2 %all_to_all.51 = f32[24,4,128]{2,1,0:T(4,128)S(1)} all-to-all(f32[24,4,128]{2,1,0:T(4,128)S(1)} %broadcast_in_dim.22), channel_id=1, replica_groups={{0,4,64,68,128,132,192,196,256,260,320,324,384,388,448,452,512,516,576,..., dimensions={0} | all-to-all | bytes 98304 | tf_op jit(solution)/shard_map/all_to_all | solution.py:38
  173.4 0.6 fusion.11
  174.7 0.6 multiply_convert_fusion
  (18 shorter events, 0.4 us)
Async XLA Ops:
  0.0 142.7 %copy-start = (bf16[4,128,256]{2,1,0:T(8,128)(2,1)S(1)}, bf16[4,128,256]{2,1,0:T(8,128)(2,1)}, u32[]{:S(2)}) copy-start(bf16[4,128,256]{2,1,0:T(8,128)(2,1)} %param.9) | copy-start | bytes 786436
  1.4 19.7 %all-to-all-start = ((bf16[8,32,128]{2,1,0:T(8,128)(2,1)}), bf16[8,32,128]{2,1,0:T(8,128)(2,1)S(1)}, u32[]{:S(2)}, u32[]{:S(2)}) async-start(bf16[8,32,128]{2,1,0:T(8,128)(2,1)} %broadcast_in_dim.18), calls=%async_computation | async-start | bytes 131072 | tf_op jit(solution)/shard_map/all_to_all | solution.py:38
  15.8 1.1 copy-start.1
  16.9 0.7 copy-start.2
  21.1 25.0 %all-to-all-start.1 = ((bf16[8,24,32,128]{3,2,1,0:T(8,128)(2,1)}), bf16[8,24,32,128]{3,2,1,0:T(8,128)(2,1)S(1)}, u32[]{:S(2)}, u32[]{:S(2)}) async-start(bf16[8,24,32,128]{3,2,1,0:T(8,128)(2,1)} %shard_map.55), calls=%async_computation.1 | async-start | bytes 3145728 | tf_op jit(solution)/shard_map/all_to_all | solution.py:38
  73.9 34.6 %copy-start.3 = (bf16[32,128]{1,0:T(8,128)(2,1)S(1)}, bf16[32,128]{1,0:T(8,128)(2,1)}, u32[]{:S(2)}) copy-start(bf16[32,128]{1,0:T(8,128)(2,1)} %param.5) | copy-start | bytes 24580

commit v5 on v4

--- a/solution.py
+++ b/solution.py
@@ -6,6 +6,7 @@
 from jax.sharding import Mesh
 from jax.sharding import PartitionSpec as P
 
+ANY = pl.BlockSpec(memory_space=pl.ANY)
 VM = pl.BlockSpec(memory_space=pltpu.VMEM)
 SM = pl.BlockSpec(memory_space=pltpu.SMEM)
 CORES = 2
@@ -39,9 +40,12 @@
 
 
 def place(layout, tiles, tile_rows, tile_count, piece):
-    def kernel(rows_ref, count_ref, tiles_ref, out_ref):
+    def kernel(rows_ref, count_ref, from_ref, out_ref, tiles_ref, sem):
         pieces = tiles_ref.shape[1] // piece
+        fetch = pltpu.make_async_copy(from_ref, tiles_ref, sem)
+        fetch.start()
         out_ref[...] = jnp.zeros_like(out_ref)
+        fetch.wait()
 
         def put(slot, carry):
             first = rows_ref[slot] * pieces
@@ -55,9 +59,10 @@
     return pl.pallas_call(
         kernel,
         out_shape=jax.ShapeDtypeStruct((layout.members, layout.squares, piece, tiles.shape[2]), tiles.dtype),
-        in_specs=[SM, SM, VM],
+        in_specs=[SM, SM, ANY],
         out_specs=VM,
-        compiler_params=pltpu.CompilerParams(vmem_limit_bytes=16 * 1024 * 1024),
+        scratch_shapes=[pltpu.VMEM(tiles.shape, tiles.dtype), pltpu.SemaphoreType.DMA],
+        compiler_params=pltpu.CompilerParams(vmem_limit_bytes=60 * 1024 * 1024),
     )(tile_rows, tile_count, tiles)
 
 

time: 176 us -> 175 us (level)
  local copies, waits for them, and re-layouts: 4.05 us -> 2.27 us
    unnamed x15 -> x11, local copies, waits for them, and re-layouts: 2.22 us -> 0.43 us
  transfers between devices with their start and end apart: 2 -> 2, of which waited for: 1 -> 1; matrix products, arithmetic and copies ran while one was open for 0% -> 0% of each run, Pallas kernels for 2% -> 3%
where the time goes in v5:
time: 175 us
  blocking collectives  134 us (77%)
  starting transfers between devices  18.2 us (10%)
  waiting for transfers between devices  10.8 us (6%)
  Pallas kernels  4.82 us (3%)
  local copies, waits for them, and re-layouts  2.27 us (1%)
  matrix products  1.89 us (1%)
    all_to_all x7, blocking collectives, exchange(): lax.all_to_all(array, ALL, 0, 0, axis_index_groups=groups, tiled=True)  124 us
    all_to_all x2, starting transfers between devices, exchange(): lax.all_to_all(array, ALL, 0, 0, axis_index_groups=groups, tiled=True)  18.2 us
    all_to_all x2, waiting for transfers between devices, exchange(): lax.all_to_all(array, ALL, 0, 0, axis_index_groups=groups, tiled=True)  10.8 us
    all_gather x1, blocking collectives, local(): lax.all_gather(in_square, ALL, axis=0, axis_index_groups=layout.x_line)  9.5 us
    pallas_call x1, Pallas kernels, place(): pl.pallas_call(kernel, out_shape=jax.ShapeDtypeStruct((layout.members, la...  4.82 us
  transfers between devices with their start and end apart: 2, of which 1 were waited for; matrix products, arithmetic and copies ran while one was open for 0% of the time, Pallas kernels for 3%

profile of v5, /device:TPU:1, one launch (start us, length us, event | category | flops | bytes accessed | tf_op | source)
XLA Modules:
  0.0 174.7 jit_solution(3412772295637504089)
XLA Ops:
  0.0 0.0 copy-start
  0.0 1.4 broadcast_in_dim.18
  1.4 13.8 %all-to-all-start = ((bf16[8,32,128]{2,1,0:T(8,128)(2,1)}), bf16[8,32,128]{2,1,0:T(8,128)(2,1)S(1)}, u32[]{:S(2)}, u32[]{:S(2)}) async-start(bf16[8,32,128]{2,1,0:T(8,128)(2,1)} %broadcast_in_dim.18), calls=%async_computation | async-start | bytes 131072 | tf_op jit(solution)/shard_map/all_to_all | solution.py:39
  15.8 4.8 %shard_map.55 = bf16[8,24,32,128]{3,2,1,0:T(8,128)(2,1)} custom-call(s32[24]{0:T(128)} %rows_ref.1, s32[1]{0:T(128)S(6)} %copy.52.count_ref, bf16[24,128,128]{2,1,0:T(8,128)(2,1)} %from_ref.1), custom_call_target="tpu_custom_call" | custom-call | tf_op jit(solution)/shard_map/pallas_call | solution.py:59
  20.6 0.0 all-to-all-done
  20.6 4.4 %all-to-all-start.1 = ((bf16[8,24,32,128]{3,2,1,0:T(8,128)(2,1)}), bf16[8,24,32,128]{3,2,1,0:T(8,128)(2,1)S(1)}, u32[]{:S(2)}, u32[]{:S(2)}) async-start(bf16[8,24,32,128]{3,2,1,0:T(8,128)(2,1)} %shard_map.55), calls=%async_computation.1 | async-start | bytes 3145728 | tf_op jit(solution)/shard_map/all_to_all | solution.py:39
  25.0 9.5 %all-gather = bf16[32,32,128]{2,1,0:T(8,128)(2,1)S(1)} all-gather(bf16[8,32,128]{2,1,0:T(8,128)(2,1)S(1)} %all-to-all-done), channel_id=2, replica_groups={{0,1,2,3},{4,5,6,7},{8,9,10,11},{12,13,14,15},{16,17,18,19},{20,21,22,2..., dimensions={0}, use_global_device_ids=true | all-gather | bytes 327680 | tf_op jit(solution)/shard_map/all_gather | solution.py:100
  34.6 10.8 %all-to-all-done.1 = bf16[8,24,32,128]{3,2,1,0:T(8,128)(2,1)S(1)} async-done(((bf16[8,24,32,128]{3,2,1,0:T(8,128)(2,1)}), bf16[8,24,32,128]{3,2,1,0:T(8,128)(2,1)S(1)}, u32[]{:S(2)}, u32[]{:S(2)}) %all-to-all-start.1) | async-done | bytes 1572896 | tf_op jit(solution)/shard_map/all_to_all | solution.py:39
  45.3 0.3 fusion.23
  45.7 0.1 constant_dynamic-update-slice_fusion.6
  45.7 0.1 constant_dynamic-update-slice_fusion.5
  45.8 0.1 constant_dynamic-update-slice_fusion.4
  45.9 0.1 constant_dynamic-update-slice_fusion.3
  46.0 0.1 constant_dynamic-update-slice_fusion.2
  46.0 0.1 constant_dynamic-update-slice_fusion.1
  46.1 0.1 constant_dynamic-update-slice_fusion
  46.2 0.6 convolution_convert_fusion.2
  46.8 26.4 %all_to_all.45 = bf16[24,32,128]{2,1,0:T(8,128)(2,1)S(1)} all-to-all(bf16[24,32,128]{2,1,0:T(8,128)(2,1)S(1)} %bitcast.204), channel_id=1, replica_groups={{0,128,256,384,512,640,16,144,272,400,528,656,32,160,288,416,544,672,48..., dimensions={0} | all-to-all | bytes 393216 | tf_op jit(solution)/shard_map/all_to_all | solution.py:39
  73.2 0.0 copy-start.1
  73.2 14.7 %all_to_all.46 = bf16[32,32,128]{2,1,0:T(8,128)(2,1)S(1)} all-to-all(bf16[32,32,128]{2,1,0:T(8,128)(2,1)S(1)} %broadcast_in_dim.19), channel_id=1, replica_groups={{0,1,2,3,64,65,66,67,8,9,10,11,72,73,74,75,4,5,6,7,68,69,70,71,12,13,14..., dimensions={0} | all-to-all | bytes 524288 | tf_op jit(solution)/shard_map/all_to_all | solution.py:39
  87.9 0.6 convolution_convert_fusion.1
  88.5 19.5 %all_to_all.47 = bf16[24,32,128]{2,1,0:T(8,128)(2,1)S(1)} all-to-all(bf16[24,32,128]{2,1,0:T(8,128)(2,1)S(1)} %bitcast.205), channel_id=1, replica_groups={{0,128,256,384,512,640,16,144,272,400,528,656,32,160,288,416,544,672,48..., dimensions={0} | all-to-all | bytes 393216 | tf_op jit(solution)/shard_map/all_to_all | solution.py:39
  108.0 0.0 copy-done.1
  108.1 14.3 %all_to_all.48 = bf16[32,32,128]{2,1,0:T(8,128)(2,1)S(1)} all-to-all(bf16[32,32,128]{2,1,0:T(8,128)(2,1)S(1)} %broadcast_in_dim.20), channel_id=1, replica_groups={{0,1,2,3,64,65,66,67,8,9,10,11,72,73,74,75,4,5,6,7,68,69,70,71,12,13,14..., dimensions={0} | all-to-all | bytes 524288 | tf_op jit(solution)/shard_map/all_to_all | solution.py:39
  122.3 0.6 convolution_convert_fusion
  122.9 19.1 %all_to_all.49 = bf16[24,32,128]{2,1,0:T(8,128)(2,1)S(1)} all-to-all(bf16[24,32,128]{2,1,0:T(8,128)(2,1)S(1)} %bitcast.203), channel_id=1, replica_groups={{0,128,256,384,512,640,16,144,272,400,528,656,32,160,288,416,544,672,48..., dimensions={0} | all-to-all | bytes 393216 | tf_op jit(solution)/shard_map/all_to_all | solution.py:39
  142.0 0.1 fusion.16
  142.1 0.0 copy-done
  142.1 0.2 fusion.24
  142.4 13.8 %all_to_all.50 = f32[32,4,128]{2,1,0:T(4,128)S(1)} all-to-all(f32[32,4,128]{2,1,0:T(4,128)S(1)} %broadcast_in_dim.21), channel_id=1, replica_groups={{0,1,2,3,8,9,10,11,16,17,18,19,24,25,26,27,32,33,34,35,40,41,42,43,48,4..., dimensions={0} | all-to-all | bytes 131072 | tf_op jit(solution)/shard_map/all_to_all | solution.py:39
  156.3 16.5 %all_to_all.51 = f32[24,4,128]{2,1,0:T(4,128)S(1)} all-to-all(f32[24,4,128]{2,1,0:T(4,128)S(1)} %broadcast_in_dim.22), channel_id=1, replica_groups={{0,4,64,68,128,132,192,196,256,260,320,324,384,388,448,452,512,516,576,..., dimensions={0} | all-to-all | bytes 98304 | tf_op jit(solution)/shard_map/all_to_all | solution.py:39
  172.8 0.6 fusion.11
  174.1 0.6 multiply_convert_fusion
  (18 shorter events, 0.4 us)
Async XLA Ops:
  0.0 142.1 %copy-start = (bf16[4,128,256]{2,1,0:T(8,128)(2,1)S(1)}, bf16[4,128,256]{2,1,0:T(8,128)(2,1)}, u32[]{:S(2)}) copy-start(bf16[4,128,256]{2,1,0:T(8,128)(2,1)} %param.9) | copy-start | bytes 786436
  1.4 19.3 %all-to-all-start = ((bf16[8,32,128]{2,1,0:T(8,128)(2,1)}), bf16[8,32,128]{2,1,0:T(8,128)(2,1)S(1)}, u32[]{:S(2)}, u32[]{:S(2)}) async-start(bf16[8,32,128]{2,1,0:T(8,128)(2,1)} %broadcast_in_dim.18), calls=%async_computation | async-start | bytes 131072 | tf_op jit(solution)/shard_map/all_to_all | solution.py:39
  20.6 24.7 %all-to-all-start.1 = ((bf16[8,24,32,128]{3,2,1,0:T(8,128)(2,1)}), bf16[8,24,32,128]{3,2,1,0:T(8,128)(2,1)S(1)}, u32[]{:S(2)}, u32[]{:S(2)}) async-start(bf16[8,24,32,128]{3,2,1,0:T(8,128)(2,1)} %shard_map.55), calls=%async_computation.1 | async-start | bytes 3145728 | tf_op jit(solution)/shard_map/all_to_all | solution.py:39
  73.2 34.8 %copy-start.1 = (bf16[32,128]{1,0:T(8,128)(2,1)S(1)}, bf16[32,128]{1,0:T(8,128)(2,1)}, u32[]{:S(2)}) copy-start(bf16[32,128]{1,0:T(8,128)(2,1)} %param.5) | copy-start | bytes 24580
